TPU v7x, 256 devices: a whole 4x4x8 slice. The times are simulated.
256 devices in a mesh: outer: 16 (over z, core), inner: 16 (over y, x).
Axes of the slice: x: 4, y: 4, z: 8, core: 2. Of those that a mesh axis runs over, the one named last changes fastest.
Arguments:
- queries: bfloat16 [2, 64, 8192], P(None, 'outer', 'inner'), may hold values from -7.5 to 7.5
- key_cache: bfloat16 [524288, 1024], P(('outer', 'inner')), may hold values from -8 to 8
- value_cache: bfloat16 [524288, 1024], P(('outer', 'inner')), may hold values from -6 to 6
- new_keys: bfloat16 [2, 64, 1024], P(None, 'outer'), may hold values from -12 to 12
- new_values: bfloat16 [2, 64, 1024], P(None, 'outer'), may hold values from -6 to 6
- lengths: int32 [64], replicated, may hold values from 32768 to 524288, as said below
Outputs:
- attended: bfloat16 [2, 64, 8192], P(None, 'outer', 'inner')
Inputs may be any that keep to these rules, and one draw needn't show every extreme that they name: `lengths`: some row uses the whole prefix and some row exactly 32768 positions.
All inputs are finite; a program needn't handle non-finite values.
Results may differ from a plain program's by a relative error of at most 0.0024.
Values may be sent and summed in bfloat16 or wider, within the bound.
A program may use at most 128 MiB of HBM per device.

v0:
```python
import math

import jax
import jax.numpy as jnp
from jax import lax
from jax.sharding import PartitionSpec as P

HQ = 64
KVH = 8
HD = 128
GROUP = 8
KBLOCK = 256
STEPS = 2


FLOOR = -1e30


def block_terms(grouped, key_block, value_block, first_position, lengths):
    extent = key_block.shape[0]
    scores = jnp.einsum(
        "rkgd,tkd->rkgt", grouped, key_block, preferred_element_type=jnp.float32
    ) / math.sqrt(HD)
    positions = first_position + jnp.arange(extent, dtype=jnp.int32)
    usable = (positions[None, :] < lengths[:, None])[:, None, None, :]
    highest = jnp.max(jnp.where(usable, scores, FLOOR), axis=-1, keepdims=True)
    shifted = jnp.where(usable, scores, highest) - highest
    weights = jnp.where(usable, jnp.exp(shifted), 0.0).astype(jnp.bfloat16)
    totals = jnp.sum(weights.astype(jnp.float32), axis=-1, keepdims=True)
    outputs = jnp.einsum("rkgt,tkd->rkgd", weights, value_block, preferred_element_type=jnp.float32)
    return (highest, totals, outputs)


def combine(first_part, second_part):
    peak_score = jnp.maximum(first_part[0], second_part[0])
    left_factor = jnp.exp(first_part[0] - peak_score)
    right_factor = jnp.exp(second_part[0] - peak_score)
    return (
        peak_score,
        left_factor * first_part[1] + right_factor * second_part[1],
        left_factor * first_part[2] + right_factor * second_part[2],
    )


def fold_first(partials):
    peak_score = jnp.max(partials[0], axis=0, keepdims=True)
    factor = jnp.exp(partials[0] - peak_score)
    return (
        peak_score,
        jnp.sum(factor * partials[1], axis=0, keepdims=True),
        jnp.sum(factor * partials[2], axis=0, keepdims=True),
    )


def finish(highest, totals, outputs, query_float, own_keys, own_values):
    own_scores = [
        jnp.sum(query_float * earlier, axis=-1, keepdims=True) / math.sqrt(HD)
        for earlier in own_keys
    ]
    peak_score = highest
    for candidate in own_scores:
        peak_score = jnp.maximum(peak_score, candidate)
    factor = jnp.exp(highest - peak_score)
    numerator = factor * outputs
    denominator = factor * totals
    for candidate, value_row in zip(own_scores, own_values):
        weight_own = jnp.exp(candidate - peak_score)
        numerator = numerator + weight_own * value_row
        denominator = denominator + weight_own
    return (numerator / denominator).reshape(numerator.shape[0], -1).astype(jnp.bfloat16)


def body(queries, key_cache, value_cache, new_keys, new_values, lengths):
    inner_count = lax.axis_size("inner")
    local_rows = queries.shape[1]
    local_heads = HQ // inner_count
    extent = key_cache.shape[0]
    block_count = extent // KBLOCK
    root = (lax.axis_index("outer") * inner_count + lax.axis_index("inner")) * extent
    key_blocks = key_cache.reshape(block_count, KBLOCK, KVH, HD)
    value_blocks = value_cache.reshape(block_count, KBLOCK, KVH, HD)
    firsts = root + jnp.arange(block_count, dtype=jnp.int32) * KBLOCK
    head_first = lax.axis_index("inner") * local_heads
    results = []
    for step_index in range(STEPS):
        head_block = lax.all_gather(queries[step_index], "inner", axis=1, tiled=True)
        all_queries = lax.all_gather(head_block, "outer", axis=0, tiled=True)
        all_rows = all_queries.shape[0]
        grouped = all_queries.reshape(all_rows, KVH, GROUP, HD)

        def visit(running, block_item):
            return (
                combine(
                    running,
                    block_terms(grouped, block_item[0], block_item[1], block_item[2], lengths),
                ),
                None,
            )

        initial = (
            jnp.full((all_rows, KVH, GROUP, 1), FLOOR, jnp.float32),
            jnp.zeros((all_rows, KVH, GROUP, 1), jnp.float32),
            jnp.zeros((all_rows, KVH, GROUP, HD), jnp.float32),
        )
        state, _ = lax.scan(visit, initial, (key_blocks, value_blocks, firsts))
        partials = (
            state[0].reshape(1, all_rows, HQ, 1),
            state[1].reshape(1, all_rows, HQ, 1),
            state[2].reshape(1, all_rows, HQ, HD),
        )
        spread = (
            lax.all_to_all(partials[0], "inner", split_axis=2, concat_axis=0, tiled=True),
            lax.all_to_all(partials[1], "inner", split_axis=2, concat_axis=0, tiled=True),
            lax.all_to_all(partials[2], "inner", split_axis=2, concat_axis=0, tiled=True),
        )
        folded = fold_first(spread)
        gathered = (
            lax.all_to_all(folded[0], "outer", split_axis=1, concat_axis=0, tiled=True),
            lax.all_to_all(folded[1], "outer", split_axis=1, concat_axis=0, tiled=True),
            lax.all_to_all(folded[2], "outer", split_axis=1, concat_axis=0, tiled=True),
        )
        owned = tuple((piece[0] for piece in fold_first(gathered)))
        query_float = queries[step_index].reshape(local_rows, local_heads, HD).astype(jnp.float32)
        own_keys = [
            lax.dynamic_slice_in_dim(
                jnp.repeat(new_keys[earlier].reshape(local_rows, KVH, HD), GROUP, axis=1),
                head_first,
                local_heads,
                1,
            ).astype(jnp.float32)
            for earlier in range(step_index + 1)
        ]
        own_values = [
            lax.dynamic_slice_in_dim(
                jnp.repeat(new_values[earlier].reshape(local_rows, KVH, HD), GROUP, axis=1),
                head_first,
                local_heads,
                1,
            ).astype(jnp.float32)
            for earlier in range(step_index + 1)
        ]
        results.append(finish(owned[0], owned[1], owned[2], query_float, own_keys, own_values))
    return jnp.stack(results)


def solution(mesh):
    placed = (
        P(None, "outer", "inner"),
        P(("outer", "inner"), None),
        P(("outer", "inner"), None),
        P(None, "outer", None),
        P(None, "outer", None),
        P(),
    )
    return jax.shard_map(
        body, mesh=mesh, in_specs=placed, out_specs=P(None, "outer", "inner"), check_vma=False
    )
```

profile of v0, /device:TPU:1, one launch (start us, length us, event | category | flops | bytes accessed | tf_op | source)
XLA Modules:
  0.0 431.2 jit_solution(17567646953118053794)
XLA Ops:
  7.3 21.4 %all-gather = bf16[1,4,8192]{2,0,1:T(2,128)(2,1)} all-gather(bf16[1,4,512]{2,0,1:T(2,128)(2,1)S(1)} %get-tuple-element.289), channel_id=2, replica_groups=mesh['outer'=16,'inner'=16] {'inner'}, dimensions={2}, use_global_device_ids=true | all-gather | bytes 69632 | tf_op jit(solution)/shard_map/all_gather | solution.py:86
  28.8 19.1 %all-gather.2 = bf16[1,4,8192]{2,0,1:T(2,128)(2,1)} all-gather(bf16[1,4,512]{2,0,1:T(2,128)(2,1)S(1)} %get-tuple-element.292), channel_id=4, replica_groups=mesh['outer'=16,'inner'=16] {'inner'}, dimensions={2}, use_global_device_ids=true | all-gather | bytes 69632 | tf_op jit(solution)/shard_map/all_gather | solution.py:86
  48.0 3.3 copy.100
  51.3 3.1 copy.55
  55.5 3.1 copy.57
  58.6 16.3 %all-gather.7.cloned.1.call-done = bf16[1,64,8192]{2,0,1:T(2,128)(2,1)} async-done(((bf16[1,4,8192]{2,0,1:T(2,128)(2,1)}), bf16[1,64,8192]{2,0,1:T(2,128)(2,1)}) %all-gather.7.cloned.1.call-update) | async-done | bytes 1048592 | tf_op jit(solution)/shard_map/all_gather | solution.py:87
  74.9 7.9 %reduce.10 = bf16[64,8192]{1,0:T(8,128)(2,1)S(1)} reduce(bf16[1,64,8192]{2,0,1:T(2,128)(2,1)} %all-gather.7.cloned.1.call-done, bf16[]{:T(256)} %constant.68), dimensions={0}, to_apply=%all-gather.1.reduce_sub_computation | reduce | bytes 2097154 | tf_op jit(solution)/shard_map/all_gather | solution.py:87
  83.7 65.3 %while.30 = (s32[]{:T(128)}, f32[64,8,8,1]{0,2,1,3:T(8,128)S(1)}, f32[64,8,8,1]{0,2,1,3:T(8,128)S(1)}, f32[64,8,8,128]{3,0,2,1:T(8,128)S(1)}, s32[8]{0:T(128)S(1...) while((s32[]{:T(128)}, f32[64,8,8,1]{0,2,1,3:T(8,128)S(1)}, ...), condition=%wide.region_3.4_spmd.clone, body=%wide.region_0.3_spmd.clone.sunk | while | flops 554746112 | bytes 19253656 | solution.py:105
  85.1 1.9 fusion.70
  88.6 3.4 fusion.73
  93.3 1.9 fusion.70
  96.7 3.4 fusion.73
  101.4 1.9 fusion.70
  104.9 3.4 fusion.73
  109.6 1.9 fusion.70
  113.0 3.4 fusion.73
  117.7 1.9 fusion.70
  121.2 3.4 fusion.73
  125.8 1.9 fusion.70
  129.3 3.4 fusion.73
  134.0 1.9 fusion.70
  137.4 3.4 fusion.73
  142.1 1.9 fusion.70
  145.6 3.4 fusion.73
  151.0 6.8 %all-to-all-start = ((f32[16,1,256]{2,1,0:T(1,128)}), f32[16,1,256]{2,1,0:T(1,128)S(1)}, u32[]{:S(2)}, u32[]{:S(2)}) async-start(f32[16,1,256]{2,1,0:T(1,128)} %reshape.419), calls=%async_computation | async-start | bytes 32768 | tf_op jit(solution)/shard_map/all_to_all | solution.py:112
  159.3 7.9 %reduce.11 = bf16[64,8192]{1,0:T(8,128)(2,1)S(1)} reduce(bf16[1,64,8192]{2,0,1:T(2,128)(2,1)} %all-gather.9.cloned.1.call-done, bf16[]{:T(256)} %constant.68), dimensions={0}, to_apply=%all-gather.3.reduce_sub_computation | reduce | bytes 2097154 | tf_op jit(solution)/shard_map/all_gather | solution.py:87
  168.1 6.7 %all-to-all-start.4 = ((f32[16,1,256]{2,1,0:T(1,128)}), f32[16,1,256]{2,1,0:T(1,128)S(1)}, u32[]{:S(2)}, u32[]{:S(2)}) async-start(f32[16,1,256]{2,1,0:T(1,128)} %reshape.421), calls=%async_computation.4 | async-start | bytes 32768 | tf_op jit(solution)/shard_map/all_to_all | solution.py:113
  174.8 79.0 %while.31 = (s32[]{:T(128)}, f32[64,8,8,1]{0,2,1,3:T(8,128)S(1)}, f32[64,8,8,1]{0,2,1,3:T(8,128)S(1)}, f32[64,8,8,128]{3,0,2,1:T(8,128)}, s32[8]{0:T(128)S(1)}, ...) while((s32[]{:T(128)}, f32[64,8,8,1]{0,2,1,3:T(8,128)S(1)}, ...), condition=%wide.region_14.15_spmd.clone, body=%wide.region_11.14_spmd.clone.sunk | while | flops 554746112 | bytes 36030928 | solution.py:105
  176.3 2.0 fusion.77
  179.9 3.4 fusion.80
  186.2 2.0 fusion.77
  189.8 3.4 fusion.80
  196.0 2.0 fusion.77
  199.7 3.4 fusion.80
  205.9 2.0 fusion.77
  209.5 3.4 fusion.80
  215.8 2.0 fusion.77
  219.4 3.4 fusion.80
  225.7 2.0 fusion.77
  229.3 3.4 fusion.80
  235.5 2.0 fusion.77
  239.1 3.4 fusion.80
  245.4 2.0 fusion.77
  249.0 3.4 fusion.80
  255.2 6.6 %all-to-all-start.10 = ((f32[16,1,256]{2,1,0:T(1,128)}), f32[16,1,256]{2,1,0:T(1,128)S(1)}, u32[]{:S(2)}, u32[]{:S(2)}) async-start(f32[16,1,256]{2,1,0:T(1,128)} %reshape.417), calls=%async_computation.10 | async-start | bytes 32768 | tf_op jit(solution)/shard_map/all_to_all | solution.py:113
  263.3 5.0 %all-to-all-done.10 = f32[16,1,256]{2,1,0:T(1,128)S(1)} async-done(((f32[16,1,256]{2,1,0:T(1,128)}), f32[16,1,256]{2,1,0:T(1,128)S(1)}, u32[]{:S(2)}, u32[]{:S(2)}) %all-to-all-start.10) | async-done | bytes 16416 | tf_op jit(solution)/shard_map/all_to_all | solution.py:113
  268.3 3.5 all-to-all-start.6
  274.1 4.1 all-to-all-done.6
  278.2 7.9 %all-to-all-start.1 = ((f32[1,64,4,1]{2,3,0,1:T(1,128)}), f32[1,64,4,1]{2,3,0,1:T(1,128)S(1)}, u32[]{:S(2)}, u32[]{:S(2)}) async-start(f32[1,64,4,1]{2,3,0,1:T(1,128)} %copy.58), calls=%async_computation.1 | async-start | bytes 65536 | tf_op jit(solution)/shard_map/all_to_all | solution.py:118
  288.4 5.0 %all-to-all-done.1 = f32[1,64,4,1]{2,3,0,1:T(1,128)S(1)} async-done(((f32[1,64,4,1]{2,3,0,1:T(1,128)}), f32[1,64,4,1]{2,3,0,1:T(1,128)S(1)}, u32[]{:S(2)}, u32[]{:S(2)}) %all-to-all-start.1) | async-done | bytes 1056 | tf_op jit(solution)/shard_map/all_to_all | solution.py:118
  293.4 3.7 all-to-all-start.5
  297.8 6.7 %all-to-all-done.5 = f32[1,64,4,1]{2,3,0,1:T(1,128)S(1)} async-done(((f32[1,64,4,1]{2,3,0,1:T(1,128)}), f32[1,64,4,1]{2,3,0,1:T(1,128)S(1)}, u32[]{:S(2)}, u32[]{:S(2)}) %all-to-all-start.5) | async-done | bytes 1056 | tf_op jit(solution)/shard_map/all_to_all | solution.py:119
  304.5 3.7 all-to-all-start.11
  308.3 7.3 %all-to-all-done.11 = f32[1,64,4,1]{2,3,0,1:T(1,128)S(1)} async-done(((f32[1,64,4,1]{2,3,0,1:T(1,128)}), f32[1,64,4,1]{2,3,0,1:T(1,128)S(1)}, u32[]{:S(2)}, u32[]{:S(2)}) %all-to-all-start.11) | async-done | bytes 1056 | tf_op jit(solution)/shard_map/all_to_all | solution.py:119
  315.5 10.3 %all_to_all.192 = f32[1,64,4,1]{2,3,0,1:T(1,128)S(1)} all-to-all(f32[1,64,4,1]{2,3,0,1:T(1,128)S(1)} %copy.73), channel_id=1, replica_groups=mesh['outer'=16,'inner'=16] {'outer'}, dimensions={1} | all-to-all | bytes 2048 | tf_op jit(solution)/shard_map/all_to_all | solution.py:118
  325.8 3.7 all-to-all-start.2
  329.6 32.9 %all-to-all-done.2 = f32[1,64,64,128]{3,1,0,2:T(8,128)S(1)} async-done(((f32[1,64,64,128]{3,1,0,2:T(8,128)}), f32[1,64,64,128]{3,1,0,2:T(8,128)S(1)}, u32[]{:S(2)}, u32[]{:S(2)}) %all-to-all-start.2) | async-done | bytes 2097184 | tf_op jit(solution)/shard_map/all_to_all | solution.py:114
  362.5 4.4 %all-to-all-start.8 = ((f32[1,64,64,128]{3,1,0,2:T(8,128)}), f32[1,64,64,128]{3,1,0,2:T(8,128)}, u32[]{:S(2)}, u32[]{:S(2)}) async-start(f32[1,64,64,128]{3,1,0,2:T(8,128)} %bitcast.274), calls=%async_computation.8 | async-start | bytes 4194304 | tf_op jit(solution)/shard_map/all_to_all | solution.py:114
  370.5 26.2 %all-to-all-done.8 = f32[1,64,64,128]{3,1,0,2:T(8,128)} async-done(((f32[1,64,64,128]{3,1,0,2:T(8,128)}), f32[1,64,64,128]{3,1,0,2:T(8,128)}, u32[]{:S(2)}, u32[]{:S(2)}) %all-to-all-start.8) | async-done | bytes 2097184 | tf_op jit(solution)/shard_map/all_to_all | solution.py:114
  396.7 5.7 %all-to-all-start.3 = ((f32[1,64,4,128]{3,2,0,1:T(4,128)}), f32[1,64,4,128]{3,2,0,1:T(4,128)S(1)}, u32[]{:S(2)}, u32[]{:S(2)}) async-start(f32[1,64,4,128]{3,2,0,1:T(4,128)} %copy.63), calls=%async_computation.3 | async-start | bytes 262144 | tf_op jit(solution)/shard_map/all_to_all | solution.py:120
  402.4 1.9 multiply_reduce_fusion
  405.0 6.5 %all-to-all-done.3 = f32[1,64,4,128]{3,2,0,1:T(4,128)S(1)} async-done(((f32[1,64,4,128]{3,2,0,1:T(4,128)}), f32[1,64,4,128]{3,2,0,1:T(4,128)S(1)}, u32[]{:S(2)}, u32[]{:S(2)}) %all-to-all-start.3) | async-done | bytes 131104 | tf_op jit(solution)/shard_map/all_to_all | solution.py:120
  411.6 3.4 all-to-all-start.9
  416.2 7.3 %all-to-all-done.9 = f32[1,64,4,128]{3,2,0,1:T(4,128)S(1)} async-done(((f32[1,64,4,128]{3,2,0,1:T(4,128)}), f32[1,64,4,128]{3,2,0,1:T(4,128)S(1)}, u32[]{:S(2)}, u32[]{:S(2)}) %all-to-all-start.9) | async-done | bytes 131104 | tf_op jit(solution)/shard_map/all_to_all | solution.py:120
  (251 shorter events, 78.7 us)
Async XLA Ops:
  6.5 68.3 %all-gather.7.cloned.1.call-start = ((), (), s32[]{:S(2)}) async-start(), calls=%async_computation.12 | async-start | bytes 2228224 | tf_op jit(solution)/shard_map/all_gather | solution.py:87
  28.7 130.5 %all-gather.9.cloned.1.call-start = ((), (), s32[]{:S(2)}) async-start(), calls=%async_computation.13 | async-start | bytes 2228224 | tf_op jit(solution)/shard_map/all_gather | solution.py:87
  51.3 3.1 copy-start
  58.6 25.1 %copy-start.4 = (s32[64]{0:T(128)S(1)}, s32[64]{0:T(128)}, u32[]{:S(2)}) copy-start(s32[64]{0:T(128)} %param.15) | copy-start | bytes 772
  149.0 25.8 %copy-start.1 = (f32[64,8,8,128]{3,0,2,1:T(8,128)}, f32[64,8,8,128]{3,0,2,1:T(8,128)S(1)}, u32[]{:S(2)}) copy-start(f32[64,8,8,128]{3,0,2,1:T(8,128)S(1)} %get-tuple-element.104) | copy-start | bytes 6291460
  151.0 17.1 %all-to-all-start = ((f32[16,1,256]{2,1,0:T(1,128)}), f32[16,1,256]{2,1,0:T(1,128)S(1)}, u32[]{:S(2)}, u32[]{:S(2)}) async-start(f32[16,1,256]{2,1,0:T(1,128)} %reshape.419), calls=%async_computation | async-start | bytes 32768 | tf_op jit(solution)/shard_map/all_to_all | solution.py:112
  168.1 87.1 %all-to-all-start.4 = ((f32[16,1,256]{2,1,0:T(1,128)}), f32[16,1,256]{2,1,0:T(1,128)S(1)}, u32[]{:S(2)}, u32[]{:S(2)}) async-start(f32[16,1,256]{2,1,0:T(1,128)} %reshape.421), calls=%async_computation.4 | async-start | bytes 32768 | tf_op jit(solution)/shard_map/all_to_all | solution.py:113
  176.3 3.6 copy-start.2
  183.4 1.4 copy-start.3
  186.2 3.6 copy-start.2
  193.2 1.4 copy-start.3
  196.0 3.6 copy-start.2
  203.1 1.4 copy-start.3
  205.9 3.6 copy-start.2
  213.0 1.4 copy-start.3
  215.8 3.6 copy-start.2
  222.8 1.4 copy-start.3
  225.6 3.6 copy-start.2
  232.7 1.4 copy-start.3
  235.5 3.6 copy-start.2
  242.6 1.4 copy-start.3
  245.4 3.6 copy-start.2
  252.4 1.4 copy-start.3
  253.8 75.7 %copy-start.5 = (bf16[2,4,1024]{2,1,0:T(4,128)(2,1)S(1)}, bf16[2,4,1024]{2,1,0:T(4,128)(2,1)}, u32[]{:S(2)}) copy-start(bf16[2,4,1024]{2,1,0:T(4,128)(2,1)} %param.13) | copy-start | bytes 49156
  253.8 75.7 %copy-start.6 = (bf16[2,4,1024]{2,1,0:T(4,128)(2,1)S(1)}, bf16[2,4,1024]{2,1,0:T(4,128)(2,1)}, u32[]{:S(2)}) copy-start(bf16[2,4,1024]{2,1,0:T(4,128)(2,1)} %param.14) | copy-start | bytes 49156
  255.2 13.1 %all-to-all-start.10 = ((f32[16,1,256]{2,1,0:T(1,128)}), f32[16,1,256]{2,1,0:T(1,128)S(1)}, u32[]{:S(2)}, u32[]{:S(2)}) async-start(f32[16,1,256]{2,1,0:T(1,128)} %reshape.417), calls=%async_computation.10 | async-start | bytes 32768 | tf_op jit(solution)/shard_map/all_to_all | solution.py:113
  268.3 9.9 %all-to-all-start.6 = ((f32[16,1,256]{2,1,0:T(1,128)}), f32[16,1,256]{2,1,0:T(1,128)S(1)}, u32[]{:S(2)}, u32[]{:S(2)}) async-start(f32[16,1,256]{2,1,0:T(1,128)} %reshape.415), calls=%async_computation.6 | async-start | bytes 32768 | tf_op jit(solution)/shard_map/all_to_all | solution.py:112
  278.2 15.2 %all-to-all-start.1 = ((f32[1,64,4,1]{2,3,0,1:T(1,128)}), f32[1,64,4,1]{2,3,0,1:T(1,128)S(1)}, u32[]{:S(2)}, u32[]{:S(2)}) async-start(f32[1,64,4,1]{2,3,0,1:T(1,128)} %copy.58), calls=%async_computation.1 | async-start | bytes 65536 | tf_op jit(solution)/shard_map/all_to_all | solution.py:118
  293.4 11.1 %all-to-all-start.5 = ((f32[1,64,4,1]{2,3,0,1:T(1,128)}), f32[1,64,4,1]{2,3,0,1:T(1,128)S(1)}, u32[]{:S(2)}, u32[]{:S(2)}) async-start(f32[1,64,4,1]{2,3,0,1:T(1,128)} %copy.66), calls=%async_computation.5 | async-start | bytes 65536 | tf_op jit(solution)/shard_map/all_to_all | solution.py:119
  304.5 11.0 %all-to-all-start.11 = ((f32[1,64,4,1]{2,3,0,1:T(1,128)}), f32[1,64,4,1]{2,3,0,1:T(1,128)S(1)}, u32[]{:S(2)}, u32[]{:S(2)}) async-start(f32[1,64,4,1]{2,3,0,1:T(1,128)} %copy.83), calls=%async_computation.11 | async-start | bytes 65536 | tf_op jit(solution)/shard_map/all_to_all | solution.py:119
  325.8 36.7 %all-to-all-start.2 = ((f32[1,64,64,128]{3,1,0,2:T(8,128)}), f32[1,64,64,128]{3,1,0,2:T(8,128)S(1)}, u32[]{:S(2)}, u32[]{:S(2)}) async-start(f32[1,64,64,128]{3,1,0,2:T(8,128)} %bitcast.273), calls=%async_computation.2 | async-start | bytes 4194304 | tf_op jit(solution)/shard_map/all_to_all | solution.py:114
  362.5 34.2 %all-to-all-start.8 = ((f32[1,64,64,128]{3,1,0,2:T(8,128)}), f32[1,64,64,128]{3,1,0,2:T(8,128)}, u32[]{:S(2)}, u32[]{:S(2)}) async-start(f32[1,64,64,128]{3,1,0,2:T(8,128)} %bitcast.274), calls=%async_computation.8 | async-start | bytes 4194304 | tf_op jit(solution)/shard_map/all_to_all | solution.py:114
  396.7 14.9 %all-to-all-start.3 = ((f32[1,64,4,128]{3,2,0,1:T(4,128)}), f32[1,64,4,128]{3,2,0,1:T(4,128)S(1)}, u32[]{:S(2)}, u32[]{:S(2)}) async-start(f32[1,64,4,128]{3,2,0,1:T(4,128)} %copy.63), calls=%async_computation.3 | async-start | bytes 262144 | tf_op jit(solution)/shard_map/all_to_all | solution.py:120
  411.6 11.9 %all-to-all-start.9 = ((f32[1,64,4,128]{3,2,0,1:T(4,128)}), f32[1,64,4,128]{3,2,0,1:T(4,128)S(1)}, u32[]{:S(2)}, u32[]{:S(2)}) async-start(f32[1,64,4,128]{3,2,0,1:T(4,128)} %copy.79), calls=%async_computation.9 | async-start | bytes 262144 | tf_op jit(solution)/shard_map/all_to_all | solution.py:120
Sparse Core Ops, SparseCore 0:
  28.9 45.9 all-gather.6
  76.7 38.0 all-gather.8
where the time goes:
time: 434 us; the launch traced here: 431 us
  waiting for transfers between devices  117 us (27%)
  matrix products  85.9 us (20%)
  other arithmetic  61.7 us (14%)
  starting transfers between devices  56.1 us (13%)
  blocking collectives  50.8 us (12%)
  local copies, waits for them, and re-layouts  44.1 us (10%)
  between operations  13.9 us (3%)
    all_to_all x2, waiting for transfers between devices, body(): lax.all_to_all(partials[2], 'inner', split_axis=2, concat_axis=0, tiled=T...  59.1 us
    dot_general x16, matrix products, block_terms(): jnp.einsum('rkgt,tkd->rkgd', weights, value_block, preferred_element_type...  54.8 us
    all_gather x2, blocking collectives, body(): lax.all_gather(queries[step_index], 'inner', axis=1, tiled=True)  40.5 us
    dot_general x16, matrix products, block_terms(): jnp.einsum('rkgd,tkd->rkgt', grouped, key_block, preferred_element_type=j...  31.1 us
    reduce_sum x16, other arithmetic, block_terms(): totals = jnp.sum(weights.astype(jnp.float32), axis=-1, keepdims=True)  24.1 us
    unnamed x33, local copies, waits for them, and re-layouts  16.3 us
    all_gather x2, waiting for transfers between devices, body(): all_queries = lax.all_gather(head_block, 'outer', axis=0, tiled=True)  16.3 us
    all_gather x2, other arithmetic, body(): all_queries = lax.all_gather(head_block, 'outer', axis=0, tiled=True)  15.7 us
  transfers between devices with their start and end apart: 13, of which 10 were waited for; matrix products, arithmetic and copies ran while one was open for 42% of the time, Pallas kernels for 0%

commit v1 on v0

v1 whole, which is shorter than its diff:
```python
import functools
import math

import jax
import jax.numpy as jnp
from jax import lax
from jax.experimental import pallas as pl
from jax.experimental.pallas import tpu as pltpu
from jax.sharding import PartitionSpec as P

HD = 128
GROUP = 8
STEPS = 2
SCALE2 = math.log2(math.e) / math.sqrt(HD)
MASKED = -1e30
LOWEST = -3e38
MESH = pl.DeviceIdType.MESH


def remote(src, dst, send_sem, recv_sem, device):
    return pltpu.make_async_remote_copy(
        src_ref=src, dst_ref=dst, send_sem=send_sem, recv_sem=recv_sem, device_id=device, device_id_type=MESH
    )


def kernel(
    sizes,
    q_ref,
    nk_hbm,
    nv_hbm,
    len_hbm,
    k_hbm,
    v_hbm,
    out_ref,
    nk_ref,
    nv_ref,
    len_ref,
    limits,
    stage,
    qbuf,
    kbuf,
    vbuf,
    qx,
    ax,
    mrun,
    mnext,
    sbuf,
    vt,
    outbuf,
    rbuf,
    zsend,
    zrecv,
    scal,
    small_sem,
    local_sem,
    kv_send,
    kv_recv,
    s1_send,
    s1_recv,
    s2_send,
    s2_recv,
    r_send,
    r_recv,
    z_send,
    z_recv,
):
    NO, NI, KL, EXT, TT, CH, QB, ROWS = sizes
    NZ = NO // 2
    QD = NZ * QB
    NQ = 4 * QD
    LT = min(128, QD)
    ZT = LT // QB
    o = lax.axis_index("outer")
    i = lax.axis_index("inner")
    z, c = o // 2, o % 2
    half_plane = NI // 2
    c_d, j_d, half_d = i // half_plane, (i % half_plane) // 2, i % 2
    mate = (z * 2 + (1 - c), i)

    def cols(head):
        return pl.ds(pl.multiple_of(head * HD, HD), HD)

    def own_kv(j, which):
        src, dst = ((k_hbm, kbuf), (v_hbm, vbuf))[which]
        return pltpu.make_async_copy(src.at[:, cols(c * KL + j)], dst.at[j, c], local_sem.at[j, which])

    def mate_kv(j, which):
        src, dst = ((k_hbm, kbuf), (v_hbm, vbuf))[which]
        return remote(
            src.at[:, cols((1 - c) * KL + j)], dst.at[j, c], kv_send.at[j, which], kv_recv.at[j, which], mate
        )

    def slot_head(k):
        return lax.rem(k + i, KL)

    def each(n, body):
        lax.fori_loop(0, n, lambda s, carry: (body(s), carry)[1], 0)

    small = [
        pltpu.make_async_copy(src, dst, small_sem.at[n])
        for n, (src, dst) in enumerate(((len_hbm, len_ref), (nk_hbm, nk_ref), (nv_hbm, nv_ref)))
    ]
    for copy in small:
        copy.start()

    @functools.partial(each, KL)
    def _(k):
        own_kv(slot_head(k), 0).start()
        own_kv(slot_head(k), 1).start()

    barrier = pltpu.get_barrier_semaphore()

    @functools.partial(each, 2 * NI - 1)
    def _(s):
        other = lax.rem(c * NI + i + s + 1, 2 * NI)
        pl.semaphore_signal(barrier, inc=1, device_id=(z * 2 + other // NI, other % NI), device_id_type=MESH)

    @functools.partial(each, NZ - 1)
    def _(s):
        pl.semaphore_signal(
            barrier, inc=1, device_id=(lax.rem(z + s + 1, NZ) * 2 + c, i), device_id_type=MESH
        )

    limits[...] = jnp.full((8, 128), 2**30, jnp.int32)
    small[0].wait()
    limits[0:1, 0:ROWS] = len_ref[...]
    lengths = limits[0:1, :]
    for u in range(2):
        first = ((z * 2 + u) * NI + i) * EXT

        def mask_tile(t, first=first, u=u):
            place = lax.broadcasted_iota(jnp.int32, (TT, 128), 0) + (first + t * TT)
            ax[u, pl.ds(pl.multiple_of(t * TT, TT), TT), :] = jnp.where(place >= lengths, MASKED, 0.0).astype(
                jnp.bfloat16
            )

        each(EXT // TT, mask_tile)
    lane = lax.broadcasted_iota(jnp.int32, (128, NQ), 1)
    row = (((lane % QD) // QB) * 2 + (lane // QD) % 2) * 4 + lane % 4
    picks = row == lax.broadcasted_iota(jnp.int32, (128, NQ), 0)
    qx[128:256, :] = jnp.where(picks, 1.0, 0.0).astype(jnp.bfloat16)
    stage[z] = q_ref[...]
    vt[128:144, :] = jnp.ones((16, TT), jnp.bfloat16)

    pl.semaphore_wait(barrier, 2 * NI - 1 + NZ - 1)

    def along_z(s):
        return remote(
            q_ref, stage.at[z], s1_send.at[s], s1_recv.at[z], (lax.rem(z + s + 1, NZ) * 2 + c, i)
        )

    each(NZ - 1, lambda s: along_z(s).start())

    @functools.partial(each, KL)
    def _(k):
        mate_kv(slot_head(k), 0).start()
        mate_kv(slot_head(k), 1).start()

    def from_z(s):
        other = lax.rem(z + s + 1, NZ)
        return remote(q_ref, stage.at[other], s1_send.at[s], s1_recv.at[other], (other * 2 + c, i))

    each(NZ - 1, lambda s: from_z(s).wait_recv())

    spread = NI // KL

    def across(s):
        k, y = s // spread, s % spread
        to = KL * y + lax.rem(j_d - k + KL, KL)
        dst = qbuf.at[j_d, half_d * 2 + c]
        sem = s2_recv.at[j_d, half_d * 2 + c]
        there = remote(stage, dst, s2_send.at[s], sem, (z * 2 + c_d, to))
        here = pltpu.make_async_copy(stage, dst, sem)
        return there, here, (to == i) & (c_d == c)

    def go(trio):
        there, here, own = trio

        @pl.when(own)
        def _():
            here.start()

        @pl.when(jnp.logical_not(own))
        def _():
            there.start()

    def gone(trio):
        there, _, own = trio

        @pl.when(jnp.logical_not(own))
        def _():
            there.wait_send()

    each(NI, lambda s: go(across(s)))

    per = EXT // TT
    blocks = NQ // CH

    def place_of(t):
        return lax.rem(c + t // per, 2), pl.ds(pl.multiple_of(lax.rem(t, per) * TT, TT), TT)

    def score(j, t, h):
        u, where = place_of(t)
        lanes = slice(h * CH, (h + 1) * CH)
        keys = jnp.concatenate([kbuf[j, u, where, :], ax[u, where, :]], axis=1)
        scores = jnp.dot(keys, qx[:, lanes], preferred_element_type=jnp.float32)
        sbuf[h % 2] = scores
        mnext[0:1, lanes] = jnp.max(scores, axis=0, keepdims=True)

    def attend(j, t):
        @pl.when(t == per - 1)
        def _():
            mate_kv(j, 0).wait_recv()
            mate_kv(j, 1).wait_recv()

        u, where = place_of(t)
        vt[0:128, :] = vbuf[j, u, where, :].T
        for h in range(blocks):
            lanes = slice(h * CH, (h + 1) * CH)
            before = mrun[0:1, lanes]
            now = jnp.maximum(before, mnext[0:1, lanes])
            if h + 1 < blocks:
                score(j, t, h + 1)
            else:
                score(j, jnp.minimum(t + 1, 2 * per - 1), 0)
            weights = jnp.exp2((sbuf[h % 2] - now) * SCALE2).astype(jnp.bfloat16)
            part = jnp.dot(vt[...], weights, preferred_element_type=jnp.float32)
            outbuf[j, :, lanes] = outbuf[j, :, lanes] * jnp.exp2((before - now) * SCALE2) + part[:136]
            mrun[0:1, lanes] = now

    def back(j, b):
        half, p = b // 2, b % 2
        to = c * half_plane + 2 * j + half
        src = outbuf.at[j, :, b * QD : (b + 1) * QD]
        there = remote(src, rbuf.at[i], r_send.at[j, b], r_recv.at[i], (z * 2 + p, to))
        here = pltpu.make_async_copy(src, rbuf.at[i], r_recv.at[i])
        return there, here, (to == i) & (c == p)

    def head_slot(k):
        j = slot_head(k)
        for b in range(4):
            pltpu.make_async_copy(stage, qbuf.at[j, b], s2_recv.at[j, b]).wait()
        qx[0:128, :] = qbuf[j].reshape(NQ, HD).T
        mrun[...] = jnp.full_like(mrun, LOWEST)
        outbuf[j] = jnp.zeros((136, NQ), jnp.float32)
        own_kv(j, 0).wait()
        own_kv(j, 1).wait()
        score(j, 0, 0)
        each(2 * per, lambda t: attend(j, t))
        outbuf[j, 129:130, :] = mrun[0:1, :]
        for b in range(4):
            go(back(j, b))

    each(KL, head_slot)

    each(
        NI,
        lambda s: pltpu.make_async_copy(rbuf.at[s], rbuf.at[s], r_recv.at[s]).wait(),
    )
    peak = lax.fori_loop(
        0, NI, lambda s, v: jnp.maximum(v, rbuf[s, 129:130, :]), jnp.full((1, QD), LOWEST, jnp.float32)
    )
    folded = lax.fori_loop(
        0,
        NI,
        lambda s, v: v + rbuf[s] * jnp.exp2((rbuf[s, 129:130, :] - peak) * SCALE2),
        jnp.zeros((136, QD), jnp.float32),
    )
    turned = folded[:128].T
    pair = jnp.concatenate(
        [jnp.broadcast_to(folded[128:129], (4, QD)), jnp.broadcast_to(peak, (4, QD))], axis=0
    )
    for d in range(NZ):
        zsend[d, 0:QB, :] = turned[d * QB : (d + 1) * QB]
        tile = (d // ZT) * LT
        zsend[d, QB : QB + 8, 0:LT] = pair[:, tile : tile + LT]

    def to_z(s):
        other = lax.rem(z + s + 1, NZ)
        return remote(zsend.at[other], zrecv.at[z], z_send.at[s], z_recv.at[z], (other * 2 + c, i))

    def of_z(s):
        other = lax.rem(z + s + 1, NZ)
        return remote(zsend.at[other], zrecv.at[other], z_send.at[s], z_recv.at[other], (other * 2 + c, i))

    each(NZ - 1, lambda s: to_z(s).start())
    zrecv[z] = zsend[z]
    each(NZ - 1, lambda s: of_z(s).wait_recv())

    for d in range(NZ):
        scal[d] = zrecv[d, QB : QB + 8, 0:LT].T
    mine = pl.ds(pl.multiple_of(lax.rem(z, ZT) * QB, QB), QB)
    sums = [scal[d, mine, 0:1] for d in range(NZ)]
    peaks = [scal[d, mine, 4:5] for d in range(NZ)]
    highest = functools.reduce(jnp.maximum, peaks)
    factors = [jnp.exp2((v - highest) * SCALE2) for v in peaks]
    total = functools.reduce(jnp.add, [f * v for f, v in zip(factors, sums)])
    result = functools.reduce(jnp.add, [f * zrecv[d, 0:QB, :] for d, f in enumerate(factors)])

    query = q_ref[...].astype(jnp.float32)
    second = lax.broadcasted_iota(jnp.int32, (QB, 1), 0) >= QB // 2
    small[1].wait()
    small[2].wait()

    def repeated(ref, e):
        four = ref[e, :, cols(i // 2)].astype(jnp.float32)
        return jnp.concatenate([four] * (QB // four.shape[0]), axis=0)

    own = [jnp.sum(query * repeated(nk_ref, e), axis=1, keepdims=True) for e in range(STEPS)]
    own[1] = jnp.where(second, own[1], LOWEST)
    top = jnp.maximum(highest, jnp.maximum(own[0], own[1]))
    factor = jnp.exp2((highest - top) * SCALE2)
    above, below = factor * result, factor * total
    for e in range(STEPS):
        w = jnp.exp2((own[e] - top) * SCALE2)
        above = above + w * repeated(nv_ref, e)
        below = below + w
    out_ref[...] = (above / below).astype(jnp.bfloat16)

    each(NZ - 1, lambda s: along_z(s).wait_send())
    each(NI, lambda s: gone(across(s)))

    def settle(j):
        mate_kv(j, 0).wait_send()
        mate_kv(j, 1).wait_send()
        for b in range(4):
            gone(back(j, b))

    each(KL, settle)
    each(NZ - 1, lambda s: to_z(s).wait_send())


def body(NO, NI, queries, key_cache, value_cache, new_keys, new_values, lengths):
    _, rows, width = queries.shape
    EXT, kv_width = key_cache.shape
    KL = kv_width // HD // 2
    heads = width // HD
    QB = STEPS * rows * heads
    NZ = NO // 2
    QD = NZ * QB
    TT = min(1024, EXT)
    CH = min(512, 2 * QD)
    LT = min(128, QD)
    q = queries.reshape(STEPS, rows, heads, HD).transpose(0, 2, 1, 3).reshape(QB, HD)
    vmem = pl.BlockSpec(memory_space=pltpu.VMEM)
    hbm = pl.BlockSpec(memory_space=pl.ANY)
    dma = pltpu.SemaphoreType.DMA
    out = pl.pallas_call(
        functools.partial(kernel, (NO, NI, KL, EXT, TT, CH, QB, lengths.shape[0])),
        out_shape=jax.ShapeDtypeStruct((QB, HD), jnp.bfloat16),
        in_specs=[vmem] + [hbm] * 5,
        out_specs=vmem,
        scratch_shapes=[
            pltpu.VMEM(new_keys.shape, jnp.bfloat16),
            pltpu.VMEM(new_values.shape, jnp.bfloat16),
            pltpu.VMEM((1, lengths.shape[0]), jnp.int32),
            pltpu.VMEM((8, 128), jnp.int32),
            pltpu.VMEM((NZ, QB, HD), jnp.bfloat16),
            pltpu.VMEM((KL, 4, NZ, QB, HD), jnp.bfloat16),
            pltpu.VMEM((KL, 2, EXT, HD), jnp.bfloat16),
            pltpu.VMEM((KL, 2, EXT, HD), jnp.bfloat16),
            pltpu.VMEM((256, 4 * QD), jnp.bfloat16),
            pltpu.VMEM((2, EXT, 128), jnp.bfloat16),
            pltpu.VMEM((8, 4 * QD), jnp.float32),
            pltpu.VMEM((8, 4 * QD), jnp.float32),
            pltpu.VMEM((2, TT, CH), jnp.float32),
            pltpu.VMEM((144, TT), jnp.bfloat16),
            pltpu.VMEM((KL, 136, 4 * QD), jnp.float32),
            pltpu.VMEM((NI, 136, QD), jnp.float32),
            pltpu.VMEM((NZ, QB + 8, HD), jnp.float32),
            pltpu.VMEM((NZ, QB + 8, HD), jnp.float32),
            pltpu.VMEM((NZ, LT, 8), jnp.float32),
            dma((3,)),
            dma((KL, 2)),
            dma((KL, 2)),
            dma((KL, 2)),
            dma((NZ,)),
            dma((NZ,)),
            dma((NI,)),
            dma((KL, 4)),
            dma((KL, 4)),
            dma((NI,)),
            dma((NZ,)),
            dma((NZ,)),
        ],
        compiler_params=pltpu.CompilerParams(
            collective_id=0, has_side_effects=True, vmem_limit_bytes=48 * 1024 * 1024
        ),
    )(q, new_keys, new_values, lengths.reshape(1, -1), key_cache, value_cache)
    return out.reshape(STEPS, heads, rows, HD).transpose(0, 2, 1, 3).reshape(queries.shape)


def solution(mesh):
    placed = (
        P(None, "outer", "inner"),
        P(("outer", "inner"), None),
        P(("outer", "inner"), None),
        P(None, "outer", None),
        P(None, "outer", None),
        P(),
    )
    return jax.shard_map(
        functools.partial(body, mesh.shape["outer"], mesh.shape["inner"]),
        mesh=mesh,
        in_specs=placed,
        out_specs=P(None, "outer", "inner"),
        check_vma=False,
    )
```

time: 434 us -> 77.1 us (0.18)
  waiting for transfers between devices: 117 us -> 0 us
  matrix products: 85.9 us -> 0 us
  Pallas kernels: 0 us -> 71.2 us
  other arithmetic: 61.7 us -> 0 us
  starting transfers between devices: 56.1 us -> 0 us
  blocking collectives: 50.8 us -> 0 us
  local copies, waits for them, and re-layouts: 44.1 us -> 5.57 us
  between operations: 13.9 us -> 0.01 us
    all_to_all x11 -> x0, waiting for transfers between devices: 101 us -> none  [the longest x2 59.1 us: body(): lax.all_to_all(partials[2], 'inner', split_axis=2, concat_axis=0, tiled=T...]
    dot_general x32 -> x0, matrix products: 85.9 us -> none  [the longest x16 54.8 us: block_terms(): jnp.einsum('rkgt,tkd->rkgd', weights, value_block, preferred_element_type...]
    pallas_call x0 -> x1, Pallas kernels: none -> 71.2 us  [body(): pl.pallas_call(functools.partial(kernel, (NO, NI, KL, EXT, TT, CH, QB, le...]
    all_to_all x11 -> x0, starting transfers between devices: 56 us -> none  [the longest x2 13.3 us: body(): lax.all_to_all(partials[1], 'inner', split_axis=2, concat_axis=0, tiled=T...]
    all_gather x2 -> x0, blocking collectives: 40.5 us -> none  [body(): lax.all_gather(queries[step_index], 'inner', axis=1, tiled=True)]
    reduce_sum x25 -> x0, other arithmetic: 27.3 us -> none  [the longest x16 24.1 us: block_terms(): totals = jnp.sum(weights.astype(jnp.float32), axis=-1, keepdims=True)]
    all_gather x2 -> x0, waiting for transfers between devices: 16.3 us -> none  [body(): all_queries = lax.all_gather(head_block, 'outer', axis=0, tiled=True)]
    all_gather x2 -> x0, other arithmetic: 15.7 us -> none  [body(): all_queries = lax.all_gather(head_block, 'outer', axis=0, tiled=True)]
  transfers between devices with their start and end apart: 13 -> 0, of which waited for: 10 -> 0; matrix products, arithmetic and copies ran while one was open for 42% -> 0% of each run, Pallas kernels for 0% -> 0%
where the time goes in v1:
time: 77.1 us; the launch traced here: 76.8 us
  Pallas kernels  71.2 us (92%)
  local copies, waits for them, and re-layouts  5.57 us (7%)
    pallas_call x1, Pallas kernels, body(): pl.pallas_call(functools.partial(kernel, (NO, NI, KL, EXT, TT, CH, QB, le...  71.2 us
    unnamed x11, local copies, waits for them, and re-layouts  5.57 us

profile of v1, /device:TPU:1, one launch (start us, length us, event | category | flops | bytes accessed | tf_op | source)
XLA Modules:
  0.0 76.8 jit_solution(11092951758673538831)
XLA Ops:
  0.0 0.0 copy-start
  0.0 2.2 %copy-done = bf16[2048,1024]{1,0:T(8,128)(2,1)S(1)} copy-done((bf16[2048,1024]{1,0:T(8,128)(2,1)S(1)}, bf16[2048,1024]{1,0:T(8,128)(2,1)}, u32[]{:S(2)}) %copy-start) | copy-done | bytes 4194328
  2.2 0.0 copy-start.1
  2.2 0.7 copy-done.1
  2.9 0.0 copy-start.2
  2.9 0.7 copy-done.2
  3.6 0.0 copy-start.3
  3.6 0.7 copy-done.3
  4.3 0.0 copy-start.4
  4.3 0.7 copy-done.4
  5.0 71.2 %shard_map.64 = bf16[32,128]{1,0:T(8,128)(2,1)S(1)} custom-call(bf16[32,128]{1,0:T(8,128)(2,1)S(1)} %bitcast.12, bf16[2,4,1024]{2,1,0:T(4,128)(2,1)S(1)} %copy-done.1, bf16[2,4,1024]{2,1,0:T(4,128)(2,1)S(1)} %copy-done.2, s32[1,64]{1,0:T(1,128)S(1)} %bitcast.13, bf16[2048,1024]{1,0:T(8,128)(2,1)S(1)} %copy-done, bf16[2048,1024]{1,0:T(8,128)(2,1)} %v_hbm.1), custom_call_target="tpu_custom_call" | custom-call | tf_op jit(solution)/shard_map/pallas_call | solution.py:348
  76.2 0.6 copy.10
Async XLA Ops:
  0.0 2.2 %copy-start = (bf16[2048,1024]{1,0:T(8,128)(2,1)S(1)}, bf16[2048,1024]{1,0:T(8,128)(2,1)}, u32[]{:S(2)}) copy-start(bf16[2048,1024]{1,0:T(8,128)(2,1)} %k_hbm.1) | copy-start | bytes 12582916
  2.2 0.7 copy-start.1
  2.9 0.7 copy-start.2
  3.6 0.7 copy-start.3
  4.3 0.7 copy-start.4
